TPU v7x, 512 devices: a whole 4x4x16 slice. The times are simulated.
512 devices in a mesh: shot: 16 (over z_hi, y, core), rcv: 32 (over z_lo, x).
Axes of the slice: x: 4, y: 4, z: 16 (z_hi: 2, z_lo: 8; z = z_hi * 8 + z_lo), core: 2. Of those that a mesh axis runs over, the one named last changes fastest.
Arguments:
- traces: bfloat16 [1024, 1024, 512], P('shot', 'rcv'), may hold values from -6 to 6
- taper_weights: float32 [512], replicated, may hold values from 0.2 to 1
Outputs:
- multiples: bfloat16 [1024, 1024, 512], P('shot', 'rcv')
All inputs are finite; a program needn't handle non-finite values.
Results may differ from a plain program's by a relative error of at most 0.0057.
Values may be sent and summed in bfloat16 or wider, within the bound.
A program may use at most 64 MiB of HBM per device.

v0:
```python
import math

import jax
import jax.numpy as jnp
from jax import lax
from jax.sharding import PartitionSpec as P

FREQ = 8


def fourier_kernel(samples_count):
    samples = jnp.arange(samples_count, dtype=jnp.int32)
    freq_bins = 1 + 3 * jnp.arange(FREQ, dtype=jnp.int32)
    phases = (
        2.0
        * math.pi
        * (freq_bins[:, None] * samples[None, :] % samples_count).astype(jnp.float32)
        / samples_count
    )
    return jnp.stack([jnp.cos(phases), -jnp.sin(phases)])


def complex_product(column_section, row_part):
    left_side = jnp.concatenate([column_section[0], column_section[1]], axis=-1)
    real_rows = jnp.concatenate([row_part[0], -row_part[1]], axis=-1)
    imag_rows = jnp.concatenate([row_part[1], row_part[0]], axis=-1)
    right_side = jnp.stack([real_rows, imag_rows])
    return jnp.einsum("frk,cfsk->cfrs", left_side, right_side, preferred_element_type=jnp.float32)


def on_device(traces, taper_weights):
    shot_rows, rcv_cols, samples_count = traces.shape
    order = shot_rows * lax.axis_size("shot")
    basis = fourier_kernel(samples_count)
    weights = (taper_weights[None, None, :] * basis / math.sqrt(samples_count)).reshape(
        2 * FREQ, samples_count
    )
    flat_traces = traces.reshape(shot_rows * rcv_cols, samples_count).astype(jnp.float32)
    spectra_flat = jnp.einsum(
        "nt,ct->cn", flat_traces, weights, precision=lax.Precision.HIGHEST
    ).astype(jnp.bfloat16)
    spectra = spectra_flat.reshape(2, FREQ, shot_rows, rcv_cols)
    columns_local = jnp.swapaxes(spectra, 2, 3)
    whole_rows = lax.all_gather(spectra, "rcv", axis=3, tiled=True)
    summed = complex_product(lax.all_gather(columns_local, "shot", axis=3, tiled=True), whole_rows)
    product = summed / math.sqrt(order)
    timed = jnp.einsum(
        "cfrs,cft->srt", product, basis, precision=lax.Precision.HIGHEST
    ) / math.sqrt(FREQ)
    return timed.astype(jnp.bfloat16)


def solution(mesh):
    placed = (P("shot", "rcv", None), P())
    return jax.shard_map(
        on_device, mesh=mesh, in_specs=placed, out_specs=P("shot", "rcv", None), check_vma=False
    )
```

profile of v0, /device:TPU:8, one launch (start us, length us, event | category | flops | bytes accessed | tf_op | source)
XLA Modules:
  0.0 387.4 jit_solution(14278276903616534583)
XLA Ops:
  6.5 0.0 copy-start
  6.5 0.0 all-gather.5.cloned.1.call-start
  6.5 0.2 fusion.27
  6.7 1.4 copy-done
  8.1 2.4 convolution_convert_fusion
  10.5 0.9 reshape.139
  11.4 0.0 all-gather.5.cloned.1.call-update
  11.5 0.0 all-gather.3.cloned.1.call-start
  11.5 1.8 copy.5
  13.3 0.0 all-gather.3.cloned.1.call-update
  13.3 120.6 %all-gather.5.cloned.1.call-done = bf16[2,8,32,1024]{2,3,1,0:T(8,128)(2,1)} async-done(((bf16[2,8,32,64]{2,3,1,0:T(8,128)(2,1)}), bf16[2,8,32,1024]{2,3,1,0:T(8,128)(2,1)}) %all-gather.5.cloned.1.call-update) | async-done | bytes 1048592 | tf_op jit(solution)/shard_map/all_gather | solution.py:45
  133.9 4.7 %slice_bitcast_fusion.1 = (bf16[8,32,1024]{1,2,0:T(8,128)(2,1)}, bf16[8,32,1024]{1,2,0:T(8,128)(2,1)}) fusion(bf16[2,8,32,1024]{2,3,1,0:T(8,128)(2,1)} %all-gather.5.cloned.1.call-done), kind=kLoop, calls=%fused_computation.8 | loop fusion | bytes 2097152 | tf_op jit(solution)/shard_map/squeeze | solution.py:24
  138.6 2.6 copy.9
  141.2 2.6 copy.10
  143.7 214.7 %all-gather.3.cloned.1.call-done = bf16[2,8,64,1024]{2,1,0,3:T(8,128)(2,1)} async-done(((bf16[2,8,64,32]{2,1,0,3:T(8,128)(2,1)}), bf16[2,8,64,1024]{2,1,0,3:T(8,128)(2,1)}) %all-gather.3.cloned.1.call-update) | async-done | bytes 2097168 | tf_op jit(solution)/shard_map/all_gather | solution.py:44
  358.4 4.5 %fusion.32 = (bf16[1,8,64,1024]{2,1,0,3:T(8,128)(2,1)}, bf16[1,8,64,1024]{2,1,0,3:T(8,128)(2,1)}) fusion(bf16[2,8,64,1024]{2,1,0,3:T(8,128)(2,1)} %all-gather.3.cloned.1.call-done), kind=kLoop, calls=%fused_computation.42 | loop fusion | bytes 4194304 | tf_op jit(solution)/shard_map/slice | solution.py:25
  362.9 2.5 copy.16
  365.4 1.0 bitcast_negate_fusion
  366.4 3.4 copy.15
  369.8 0.0 copy-start.1
  369.8 0.0 copy-start.2
  369.8 2.3 maximum_bitcast_fusion
  372.1 0.0 copy-done.1
  372.1 0.0 copy-done.2
  372.1 2.2 fusion.9
  374.3 3.8 fusion.5
  378.1 2.5 copy.12
  (1 shorter events, 0.0 us)
Async XLA Ops:
  6.5 1.6 copy-start
  6.5 127.4 %all-gather.5.cloned.1.call-start = ((), (), s32[]{:S(2)}) async-start(), calls=%async_computation.1 | async-start | bytes 4456448 | tf_op jit(solution)/shard_map/all_gather | solution.py:45
  11.5 346.9 %all-gather.3.cloned.1.call-start = ((), (), s32[]{:S(2)}) async-start(), calls=%async_computation | async-start | bytes 4325376 | tf_op jit(solution)/shard_map/all_gather | solution.py:44
  369.8 2.3 copy-start.1
  369.8 2.3 copy-start.2
Sparse Core Ops, SparseCore 0:
  11.6 122.2 all-gather.4
  136.0 222.3 all-gather.2
where the time goes:
time: 388 us; the launch traced here: 387 us
  waiting for transfers between devices  335 us (86%)
  local copies, waits for them, and re-layouts  26.8 us (7%)
  between operations  13.4 us (3%)
  matrix products  8.38 us (2%)
    all_gather x1, waiting for transfers between devices, on_device(): whole_rows = lax.all_gather(spectra, 'rcv', axis=3, tiled=True)  215 us
    all_gather x1, waiting for transfers between devices, on_device(): lax.all_gather(columns_local, 'shot', axis=3, tiled=True)  121 us
    squeeze x3, local copies, waits for them, and re-layouts, complex_product(): left_side = jnp.concatenate([column_section[0], column_section[1]], axis=-1)  9.81 us
  transfers between devices with their start and end apart: 2, of which 2 were waited for; matrix products, arithmetic and copies ran while one was open for 3% of the time, Pallas kernels for 0%

commit v1 on v0

v1 whole, which is shorter than its diff:
```python
import functools
import math

import jax
import jax.numpy as jnp
import numpy as np
from jax import lax
from jax.experimental import pallas as pl
from jax.experimental.pallas import tpu as pltpu
from jax.sharding import PartitionSpec as P

FREQ = 8
MESH = pl.DeviceIdType.MESH
BF16, F32 = jnp.bfloat16, jnp.float32


def fourier_table(samples_count):
    samples = np.arange(samples_count)
    freq_bins = 1 + 3 * np.arange(FREQ)
    phases = 2.0 * math.pi * (freq_bins[:, None] * samples[None, :] % samples_count) / samples_count
    return np.concatenate([np.cos(phases), -np.sin(phases)]).astype(np.float32)


def place():
    shot, rcv = lax.axis_index("shot"), lax.axis_index("rcv")
    return lax.rem(rcv, 4), lax.rem(shot // 2, 4), shot // 8 * 8 + rcv // 4, lax.rem(shot, 2)


def device(x, y, z, core):
    return (z // 8 * 8 + y * 2 + core, lax.rem(z, 8) * 4 + x)


def ring(value, size):
    return lax.rem(value + size, size)


def split_in_two(value):
    high = value.astype(BF16)
    return high, (value - high.astype(F32)).astype(BF16)


def swap_quarters(tiles):
    quarter = lax.broadcasted_iota(jnp.int32, tiles[0].shape, 1) // 32
    out = []
    for j in range(4):
        total = None
        for i in range(4):
            shift = 32 * ((i - j) % 4)
            moved = pltpu.roll(tiles[i], shift, 1) if shift else tiles[i]
            total = moved if total is None else jnp.where(quarter == i, moved, total)
        out.append(total)
    return out


def product_kernel(
    traces, taper, basis, m_ref,
    tr, by_s, zsend, zin, own, a_buf, b_buf, c_out, c_in, c_own, zret,
    t_sem, zs_sem, zr_sem, as_sem, ar_sem, bs_sem, br_sem, cs_sem, cr_sem, rs_sem, rr_sem,
):
    x, y, z, core = place()
    pair = z // 2
    active = lax.rem(z, 2) == 0
    x_half, x_core = lax.rem(x, 2), x // 2
    samples = traces.shape[-1]

    def remote(src, dst, send, recv, target):
        return pltpu.make_async_remote_copy(
            src_ref=src, dst_ref=dst, send_sem=send, recv_sem=recv, device_id=target, device_id_type=MESH
        )

    barrier = pltpu.get_barrier_semaphore()

    def greet(target):
        pl.semaphore_signal(barrier, inc=1, device_id=target, device_id_type=MESH)

    @pl.when(active)
    def _():
        for step in (8, 7, 9, 6, 10, 5, 11, 4, 12, 3, 13, 2, 14, 1, 15):
            greet(device(x, y, lax.rem(z + step, 16), core))
        for step in (2, 1, 3):
            for other in (0, 1):
                greet(device(lax.rem(x + step, 4), y, z, other))
            greet(device(x, lax.rem(y + step, 4), z, core))
        greet(device(x, y, z, 1 - core))

    @pl.when(jnp.logical_not(active))
    def _():
        for step in (4, 3, 5, 2, 6, 1, 7, 0):
            greet(device(x, y, 2 * lax.rem(pair + step, 8), core))

    chunks = t_sem.shape[0]
    per_chunk = 16 // chunks

    def load(chunk):
        rows = pl.ds(chunk * per_chunk, per_chunk)
        return pltpu.make_async_copy(traces.at[:, rows], tr.at[:, rows], t_sem.at[chunk])

    for chunk in range(chunks):
        load(chunk).start()
    high, low = split_in_two(basis[...] * taper[...] / math.sqrt(samples))
    weights = jnp.concatenate([high, low])
    for s in range(0, 16, 2):
        if s % per_chunk == 0:
            load(s // per_chunk).wait()
        block = jnp.concatenate([tr[:, s], tr[:, s + 1]]).reshape(256, samples)
        both = lax.dot_general(weights, block, (((1,), (1,)), ((), ())), preferred_element_type=F32)
        summed = both[:16] + both[16:]
        by_s[pl.ds(s * 16, 16)] = summed[:, :128]
        by_s[pl.ds(s * 16 + 16, 16)] = summed[:, 128:]
    for freq in range(FREQ):
        for part in range(2):
            zsend[freq, part] = by_s[pl.ds(part * FREQ + freq, 16, stride=16), :].astype(BF16)

    @pl.when(active)
    def _():
        pl.semaphore_wait(barrier, 15 + 9 + 1)

    @pl.when(jnp.logical_not(active))
    def _():
        pl.semaphore_wait(barrier, 8)

    far_first = (4, 3, 5, 2, 6, 1, 7, 0)

    def to_plane(step):
        freq = lax.rem(pair + step, 8)
        return remote(
            zsend.at[freq], zin.at[z], zs_sem.at[step], zr_sem.at[z], device(x, y, 2 * freq, core)
        )

    for step in far_first[:-1]:
        to_plane(step).start()

    @pl.when(jnp.logical_not(active))
    def _():
        to_plane(0).start()

    def product_of_plane():
        zin[z] = zsend[pair]

        def a_copy(group, step):
            return remote(
                own.at[group], a_buf.at[x_half, group, core], as_sem.at[group, step], ar_sem.at[x_half, core, group],
                device(lax.rem(x + step, 4), y, z, x_core),
            )

        def b_copy(group, step):
            return remote(
                own.at[group], b_buf.at[group, :, :, y], bs_sem.at[group, step], br_sem.at[y, group],
                device(x, lax.rem(y + step, 4), z, core),
            )

        @pl.loop(0, 4)
        def _(index):
            group = lax.rem(z // 4 + (index ^ (index // 2)), 4)
            for i in range(4):
                source = group * 4 + i

                @pl.when(source != z)
                def _():
                    remote(
                        zsend.at[0], zin.at[source], zs_sem.at[0], zr_sem.at[source], device(x, y, z, core)
                    ).wait_recv()

            for part in range(2):
                tiles = swap_quarters([zin[group * 4 + i, part].astype(F32) for i in range(4)])
                for j in range(4):
                    tile = tiles[j].astype(BF16)
                    rows = pl.ds(j % 2 * 16, 16)
                    own[group, part, j // 2, rows] = tile
                    b_buf[group, part, j // 2, y, rows] = tile
            for step in (2, 1, 3):
                a_copy(group, step).start()
                b_copy(group, step).start()

            @pl.when(x_core != core)
            def _():
                a_copy(group, 0).start()

            @pl.when(x_core == core)
            def _():
                a_buf[x_half, group, core] = own[group]

        @pl.loop(0, 4)
        def _(group):
            for half in range(2):
                for other in range(2):

                    @pl.when(jnp.logical_or(x != 2 * core + half, other != core))
                    def _():
                        remote(
                            own.at[0], a_buf.at[half, group, other], as_sem.at[0, 0], ar_sem.at[half, other, group],
                            device(x, y, z, core),
                        ).wait_recv()

            for step in (1, 2, 3):
                row = lax.rem(y + step, 4)
                remote(
                    own.at[0], b_buf.at[group, :, :, row], bs_sem.at[0, 0], br_sem.at[row, group],
                    device(x, y, z, core),
                ).wait_recv()

        def right(part):
            return jnp.concatenate(
                [
                    jnp.concatenate(
                        [b_buf[2 * deep + wide, part, half].reshape(128, 128) for wide in range(2)], axis=1
                    )
                    for half in range(2)
                    for deep in range(2)
                ]
            )

        def left(rows_of, part, upper):
            return jnp.concatenate(
                [
                    a_buf[half, 2 * upper + deep, rows_of, part].reshape(64, 128)
                    for half in range(2)
                    for deep in range(2)
                ],
                axis=1,
            )

        def multiply(rows_of, out):
            rows = jnp.concatenate([left(rows_of, part, upper) for part in range(2) for upper in range(2)])
            by_real = jnp.dot(rows, right(0), preferred_element_type=F32)
            by_imag = jnp.dot(rows, right(1), preferred_element_type=F32)
            out[0] = by_real[:128] - by_imag[128:]
            out[1] = by_imag[:128] + by_real[128:]

        to_partner = remote(c_out, c_in, cs_sem, cr_sem, device(x, y, z, 1 - core))
        multiply(1 - core, c_out)
        to_partner.start()
        multiply(core, c_own)
        to_partner.wait_recv()

        def back(target, slot):
            return remote(
                zret.at[target], m_ref.at[pair], rs_sem.at[slot], rr_sem.at[pair], device(x, y, target, core)
            )

        @pl.loop(0, 4)
        def _(index):
            group = lax.rem(z // 4 + 2 + (index ^ (index // 2)), 4)
            upper, wide = group // 2, lax.rem(group, 2)
            lanes = pl.ds(pl.multiple_of(wide * 128, 128), 128)
            for part in range(2):
                tiles = []
                for j in range(4):
                    rows = pl.ds(pl.multiple_of(upper * 64 + j * 16, 16), 16)
                    tiles.append(c_own[part, rows, lanes] + c_in[part, rows, lanes])
                tiles = swap_quarters(tiles)
                for i in range(4):
                    zret[group * 4 + i, part] = (tiles[i] * (1.0 / 32.0)).astype(BF16)
            for i in range(4):
                target = group * 4 + i

                @pl.when(target != z)
                def _():
                    back(target, target).start()

        m_ref[pair] = zret[z]
        to_partner.wait_send()

        @pl.loop(0, 4)
        def _(group):
            for step in (1, 2, 3):
                a_copy(group, step).wait_send()
                b_copy(group, step).wait_send()

            @pl.when(x_core != core)
            def _():
                a_copy(group, 0).wait_send()

        @pl.loop(0, 16)
        def _(target):
            @pl.when(target != z)
            def _():
                back(target, target).wait_send()

    pl.when(active)(product_of_plane)

    for step in far_first[:-1]:
        to_plane(step).wait_send()

    @pl.when(jnp.logical_not(active))
    def _():
        to_plane(0).wait_send()

    for freq in range(FREQ):

        @pl.when(2 * freq != z)
        def _():
            remote(
                zret.at[0], m_ref.at[freq], rs_sem.at[0], rr_sem.at[freq], device(x, y, z, core)
            ).wait_recv()


def time_kernel(m_ref, basis, out, by_cf):
    @pl.when(pl.program_id(0) == 0)
    def _():
        for freq in range(FREQ):
            for part in range(2):
                by_cf[pl.ds((part * FREQ + freq) * 16, 16)] = m_ref[freq, part].astype(F32)

    high, low = split_in_two(basis[...] * (1.0 / math.sqrt(FREQ)))
    weights = jnp.concatenate([high, low])
    width = out.shape[1]
    for i in range(width):
        s = pl.program_id(0) * width + i
        rows = by_cf[pl.ds(s, 16, stride=16), :].astype(BF16)
        rows = jnp.concatenate([rows, rows])
        timed = lax.dot_general(rows, weights, (((0,), (0,)), ((), ())), preferred_element_type=F32)
        out[:, i] = timed.astype(BF16).reshape(4, 32, out.shape[-1])


def on_device(traces, taper_weights):
    shots, receivers, samples = traces.shape
    table = fourier_table(samples)
    vmem = pl.BlockSpec(memory_space=pltpu.VMEM)
    dma = pltpu.SemaphoreType.DMA
    product = pl.pallas_call(
        product_kernel,
        out_shape=jax.ShapeDtypeStruct((FREQ, 2, 16, 128), BF16),
        in_specs=[pl.BlockSpec(memory_space=pl.ANY), vmem, vmem],
        out_specs=vmem,
        scratch_shapes=[
            pltpu.VMEM((4, 16, receivers, samples), BF16),
            pltpu.VMEM((256, 128), F32),
            pltpu.VMEM((FREQ, 2, 16, 128), BF16),
            pltpu.VMEM((16, 2, 16, 128), BF16),
            pltpu.VMEM((4, 2, 2, 32, 128), BF16),
            pltpu.VMEM((2, 4, 2, 2, 2, 32, 128), BF16),
            pltpu.VMEM((4, 2, 2, 4, 32, 128), BF16),
            pltpu.VMEM((2, 128, 256), F32),
            pltpu.VMEM((2, 128, 256), F32),
            pltpu.VMEM((2, 128, 256), F32),
            pltpu.VMEM((16, 2, 16, 128), BF16),
            dma((4,)), dma((8,)), dma((16,)), dma((4, 4)), dma((2, 2, 4)), dma((4, 4)), dma((4, 4)),
            dma, dma, dma((16,)), dma((8,)),
        ],
        compiler_params=pltpu.CompilerParams(
            collective_id=0, has_side_effects=True, vmem_limit_bytes=32 << 20
        ),
        name="product",
    )(traces.reshape(4, 16, receivers, samples), taper_weights.reshape(1, samples), table)
    steps = 4
    timed = pl.pallas_call(
        time_kernel,
        grid=(steps,),
        out_shape=jax.ShapeDtypeStruct((4, 16, receivers, samples), BF16),
        in_specs=[
            pl.BlockSpec((FREQ, 2, 16, 128), lambda i: (0, 0, 0, 0)),
            pl.BlockSpec((2 * FREQ, samples), lambda i: (0, 0)),
        ],
        out_specs=pl.BlockSpec((4, 16 // steps, receivers, samples), lambda i: (0, i, 0, 0)),
        scratch_shapes=[pltpu.VMEM((256, 128), F32)],
        compiler_params=pltpu.CompilerParams(vmem_limit_bytes=32 << 20),
        name="back_to_time",
    )(product, table)
    return timed.reshape(shots, receivers, samples)


def solution(mesh):
    placed = (P("shot", "rcv", None), P())
    return jax.shard_map(
        on_device, mesh=mesh, in_specs=placed, out_specs=P("shot", "rcv", None), check_vma=False
    )
```

time: 388 us -> 43.9 us (0.11)
  the two profiles are of different devices: /device:TPU:8 before, /device:TPU:1 now
where the time goes in v1:
time: 43.9 us; the launch traced here: 43.7 us
  Pallas kernels  40.7 us (93%)
  local copies, waits for them, and re-layouts  3.03 us (7%)
    pallas_call x1, Pallas kernels, on_device(): pl.pallas_call(product_kernel, out_shape=jax.ShapeDtypeStruct((FREQ, 2, 1...  38 us
    unnamed x6, local copies, waits for them, and re-layouts  3.03 us
    pallas_call x1, Pallas kernels, on_device(): pl.pallas_call(time_kernel, grid=(steps,), out_shape=jax.ShapeDtypeStruct...  2.63 us

profile of v1, /device:TPU:1, one launch (start us, length us, event | category | flops | bytes accessed | tf_op | source)
XLA Modules:
  0.0 43.7 jit_solution(16449876166040144760)
XLA Ops:
  0.0 0.0 copy-start
  0.0 1.6 %copy-done = bf16[64,32,512]{2,1,0:T(8,128)(2,1)S(1)} copy-done((bf16[64,32,512]{2,1,0:T(8,128)(2,1)S(1)}, bf16[64,32,512]{2,1,0:T(8,128)(2,1)}, u32[]{:S(2)}) %copy-start) | copy-done | bytes 2097176
  1.6 0.0 copy-start.1
  1.6 0.8 %copy-done.1 = f32[16,512]{1,0:T(8,128)S(1)} copy-done((f32[16,512]{1,0:T(8,128)S(1)}, f32[16,512]{1,0:T(8,128)}, u32[]{:S(2)}) %copy-start.1) | copy-done | bytes 32792
  2.4 0.0 copy-start.2
  2.4 0.7 %copy-done.2 = f32[512]{0:T(512)S(1)} copy-done((f32[512]{0:T(512)S(1)}, f32[512]{0:T(512)}, u32[]{:S(2)}) %copy-start.2) | copy-done | bytes 2072
  3.0 38.0 %product.1.m_ref = bf16[8,2,16,128]{3,2,1,0:T(8,128)(2,1)S(1)} custom-call(bf16[4,16,32,512]{3,2,1,0:T(8,128)(2,1)S(1)} %bitcast.3, f32[1,512]{1,0:T(1,128)S(1)} %bitcast.4, f32[16,512]{1,0:T(8,128)S(1)} %copy-done.1), custom_call_target="tpu_custom_call" | custom-call | tf_op jit(solution)/shard_map/product/pallas_call | solution.py:321
  41.1 2.6 %back_to_time.1 = bf16[4,16,32,512]{3,2,1,0:T(8,128)(2,1)} custom-call(bf16[8,2,16,128]{3,2,1,0:T(8,128)(2,1)S(1)} %product.1.m_ref, f32[16,512]{1,0:T(8,128)S(1)} %copy-done.1), custom_call_target="tpu_custom_call" | custom-call | tf_op jit(solution)/shard_map/back_to_time/pallas_call | solution.py:347
Async XLA Ops:
  0.0 1.6 %copy-start = (bf16[64,32,512]{2,1,0:T(8,128)(2,1)S(1)}, bf16[64,32,512]{2,1,0:T(8,128)(2,1)}, u32[]{:S(2)}) copy-start(bf16[64,32,512]{2,1,0:T(8,128)(2,1)} %param.3) | copy-start | bytes 6291460
  1.6 0.8 %copy-start.1 = (f32[16,512]{1,0:T(8,128)S(1)}, f32[16,512]{1,0:T(8,128)}, u32[]{:S(2)}) copy-start(f32[16,512]{1,0:T(8,128)} %constant.2.clone.basis) | copy-start | bytes 98308
  2.4 0.7 %copy-start.2 = (f32[512]{0:T(512)S(1)}, f32[512]{0:T(512)}, u32[]{:S(2)}) copy-start(f32[512]{0:T(512)} %param.4) | copy-start | bytes 6148

commit v2 on v1

v2 whole, which is shorter than its diff:
```python
import functools
import math

import jax
import jax.numpy as jnp
import numpy as np
from jax import lax
from jax.experimental import pallas as pl
from jax.experimental.pallas import tpu as pltpu
from jax.sharding import PartitionSpec as P

FREQ = 8
MESH = pl.DeviceIdType.MESH
BF16, F32 = jnp.bfloat16, jnp.float32


def fourier_table(samples_count):
    samples = np.arange(samples_count)
    freq_bins = 1 + 3 * np.arange(FREQ)
    phases = 2.0 * math.pi * (freq_bins[:, None] * samples[None, :] % samples_count) / samples_count
    return np.concatenate([np.cos(phases), -np.sin(phases)]).astype(np.float32)


def fourier_rows(samples_count):
    row = lax.broadcasted_iota(jnp.int32, (2 * FREQ, samples_count), 0)
    sample = lax.broadcasted_iota(jnp.int32, (2 * FREQ, samples_count), 1)
    quarters = 1 + row // FREQ
    turns = (1 + 3 * (row % FREQ)) * sample + quarters * (samples_count // 4) + samples_count // 2
    turns = turns % samples_count - samples_count // 2
    return jnp.sin(turns.astype(F32) * (2.0 * math.pi / samples_count))


def place():
    shot, rcv = lax.axis_index("shot"), lax.axis_index("rcv")
    return lax.rem(rcv, 4), lax.rem(shot // 2, 4), shot // 8 * 8 + rcv // 4, lax.rem(shot, 2)


def device(x, y, z, core):
    return (z // 8 * 8 + y * 2 + core, lax.rem(z, 8) * 4 + x)


def ring(value, size):
    return lax.rem(value + size, size)


def split_in_two(value):
    high = value.astype(BF16)
    return high, (value - high.astype(F32)).astype(BF16)


def swap_quarters(tiles):
    quarter = lax.broadcasted_iota(jnp.int32, tiles[0].shape, 1) // 32
    out = []
    for j in range(4):
        total = None
        for i in range(4):
            shift = 32 * ((i - j) % 4)
            moved = pltpu.roll(tiles[i], shift, 1) if shift else tiles[i]
            total = moved if total is None else jnp.where(quarter == i, moved, total)
        out.append(total)
    return out


def product_kernel(
    traces, taper_any, m_ref,
    tr, taper, by_s, zsend, zin, own, a_buf, b_buf, early, c_out, c_in, c_own, zret,
    t_sem, w_sem, m_sem, zs_sem, zr_sem, as_sem, ar_sem, bs_sem, br_sem, cs_sem, cr_sem, rs_sem, rr_sem,
):
    x, y, z, core = place()
    in_plane = z < FREQ
    x_half, x_core = lax.rem(x, 2), x // 2
    samples = traces.shape[-1]

    def remote(src, dst, send, recv, target):
        return pltpu.make_async_remote_copy(
            src_ref=src, dst_ref=dst, send_sem=send, recv_sem=recv, device_id=target, device_id_type=MESH
        )

    def arrived(ref, sem):
        remote(ref, ref, sem, sem, device(x, y, z, core)).wait_recv()

    def sent(ref, sem):
        remote(ref, ref, sem, sem, device(x, y, z, core)).wait_send()

    chunks = t_sem.shape[0]
    per_chunk = 16 // chunks

    def load(chunk):
        rows = pl.ds(chunk * per_chunk, per_chunk)
        return pltpu.make_async_copy(traces.at[:, rows], tr.at[:, rows], t_sem.at[chunk])

    load_taper = pltpu.make_async_copy(taper_any, taper, w_sem)
    load_taper.start()
    for chunk in range(chunks):
        load(chunk).start()

    barrier = pltpu.get_barrier_semaphore()

    def greet(target):
        pl.semaphore_signal(barrier, inc=1, device_id=target, device_id_type=MESH)

    @pl.when(in_plane)
    def _():
        for step in (8, 7, 9, 6, 10, 5, 11, 4, 12, 3, 13, 2, 14, 1, 15):
            greet(device(x, y, lax.rem(z + step, 16), core))
        for step in (2, 1, 3):
            for other in (0, 1):
                greet(device(lax.rem(x + step, 4), y, z, other))
            greet(device(x, lax.rem(y + step, 4), z, core))
        greet(device(x, y, z, 1 - core))

    rows = fourier_rows(samples)
    load_taper.wait()
    high, low = split_in_two(rows * taper[...] / math.sqrt(samples))
    weights = jnp.concatenate([high, low])
    for s in range(0, 16, 2):
        if s % per_chunk == 0:
            load(s // per_chunk).wait()
        block = jnp.concatenate([tr[:, s], tr[:, s + 1]]).reshape(256, samples)
        both = lax.dot_general(weights, block, (((1,), (1,)), ((), ())), preferred_element_type=F32)
        summed = both[:16] + both[16:]
        by_s[pl.ds(s * 16, 16)] = summed[:, :128]
        by_s[pl.ds(s * 16 + 16, 16)] = summed[:, 128:]
    for freq in range(FREQ):
        for part in range(2):
            zsend[freq, part] = by_s[pl.ds(part * FREQ + freq, 16, stride=16), :].astype(BF16)

    @pl.when(in_plane)
    def _():
        pl.semaphore_wait(barrier, 7 + 9 + 1)

    @pl.when(jnp.logical_not(in_plane))
    def _():
        pl.semaphore_wait(barrier, 8)

    others_first = (1, 7, 2, 6, 3, 5, 4)

    def to_plane(step):
        freq = lax.rem(z + step, 8)
        return remote(zsend.at[freq], zin.at[z], zs_sem, zr_sem.at[z // 4], device(x, y, freq, core))

    @pl.when(jnp.logical_not(in_plane))
    def _():
        to_plane(0).start()

    for step in others_first:
        to_plane(step).start()

    def product_of_plane():
        zin[z] = zsend[z]

        def a_copy(group, step):
            return remote(
                own.at[group], a_buf.at[x_half, group, core], as_sem.at[0 if step else 1], ar_sem.at[group // 2],
                device(lax.rem(x + step, 4), y, z, x_core),
            )

        def b_copy(group, step):
            return remote(
                own.at[group], b_buf.at[group, :, :, y], bs_sem, br_sem.at[group // 2],
                device(x, lax.rem(y + step, 4), z, core),
            )

        def arrange(group):
            @pl.when(group == z // 4)
            def _():
                arrived(zin.at[pl.ds(0, 3)], zr_sem.at[group])

            @pl.when(group != z // 4)
            def _():
                arrived(zin.at[pl.ds(0, 4)], zr_sem.at[group])

            for part in range(2):
                tiles = swap_quarters([zin[group * 4 + i, part].astype(F32) for i in range(4)])
                for j in range(4):
                    tile = tiles[j].astype(BF16)
                    rows = pl.ds(j % 2 * 16, 16)
                    own[group, part, j // 2, rows] = tile
                    b_buf[group, part, j // 2, y, rows] = tile
            for step in (2, 1, 3):
                b_copy(group, step).start()
            for step in (2, 1, 3):
                a_copy(group, step).start()

            @pl.when(x_core != core)
            def _():
                a_copy(group, 0).start()

            @pl.when(x_core == core)
            def _():
                a_buf[x_half, group, core] = own[group]

        def await_a(late):
            @pl.when(x_core == core)
            def _():
                arrived(a_buf.at[:, pl.ds(0, 3), 0], ar_sem.at[late])

            @pl.when(x_core != core)
            def _():
                arrived(a_buf.at[:, pl.ds(0, 2)], ar_sem.at[late])

        def await_b(late):
            arrived(a_buf.at[:, pl.ds(0, 3), 0], br_sem.at[late])

        def right(part, deep):
            return jnp.concatenate(
                [
                    jnp.concatenate(
                        [b_buf[2 * deep + wide, part, half].reshape(128, 128) for wide in range(2)], axis=1
                    )
                    for half in range(2)
                ]
            )

        def left(upper, deep):
            return jnp.concatenate(
                [
                    jnp.concatenate(
                        [a_buf[half, 2 * upper + deep, rows_of, part].reshape(64, 128) for half in range(2)], axis=1
                    )
                    for rows_of in (1 - core, core)
                    for part in range(2)
                ]
            )

        def multiply(upper, deep):
            rows = left(upper, deep)
            by_real = jnp.dot(rows, right(0, deep), preferred_element_type=F32)
            by_imag = jnp.dot(rows, right(1, deep), preferred_element_type=F32)
            out = []
            for at in (0, 128):
                out.append(by_real[at : at + 64] - by_imag[at + 64 : at + 128])
                out.append(by_imag[at : at + 64] + by_real[at + 64 : at + 128])
            return out

        def to_partner(upper):
            return remote(
                c_out.at[upper], c_in.at[upper], cs_sem.at[upper], cr_sem.at[upper], device(x, y, z, 1 - core)
            )

        def back(target):
            return remote(
                zret.at[target], m_ref.at[z], rs_sem, rr_sem, device(x, y, target, core)
            )

        def send_back(upper):
            for wide in range(2):
                group = 2 * upper + wide
                for part in range(2):
                    tiles = []
                    for j in range(4):
                        at = (upper, part, pl.ds(j * 16, 16), pl.ds(wide * 128, 128))
                        tiles.append(c_own[at] + c_in[at])
                    tiles = swap_quarters(tiles)
                    for i in range(4):
                        zret[group * 4 + i, part] = (tiles[i] * (1.0 / 32.0)).astype(BF16)
                for i in range(4):
                    target = group * 4 + i

                    @pl.when(target != z)
                    def _():
                        back(target).start()

        @pl.loop(0, 2)
        def _(index):
            arrange((z // 4) ^ index)

        await_a(0)
        await_b(0)
        for k, value in enumerate(multiply(0, 0)):
            early[k] = value

        @pl.loop(0, 2)
        def _(index):
            arrange(2 + (1 - z // 4) ^ index)

        await_b(1)
        values = multiply(0, 1)
        for part in range(2):
            c_out[0, part] = early[part] + values[part]
        to_partner(0).start()
        for part in range(2):
            c_own[0, part] = early[2 + part] + values[2 + part]
        to_partner(0).wait_recv()
        send_back(0)
        keep = pltpu.make_async_copy(zret.at[z], m_ref.at[z], m_sem)
        keep.start()

        await_a(1)
        values = [a + b for a, b in zip(multiply(1, 0), multiply(1, 1))]
        for part in range(2):
            c_out[1, part] = values[part]
        to_partner(1).start()
        for part in range(2):
            c_own[1, part] = values[2 + part]
        to_partner(1).wait_recv()
        send_back(1)

        keep.wait()
        to_partner(0).wait_send()
        to_partner(1).wait_send()
        sent(a_buf.at[:, pl.ds(0, 3)], as_sem.at[0])
        sent(a_buf.at[:, pl.ds(0, 3)], bs_sem)

        @pl.when(x_core != core)
        def _():
            sent(a_buf.at[0, :, 0], as_sem.at[1])

        sent(zret.at[pl.ds(0, 15)], rs_sem)

    pl.when(in_plane)(product_of_plane)

    @pl.when(in_plane)
    def _():
        sent(zsend.at[pl.ds(0, 7)], zs_sem)

    @pl.when(jnp.logical_not(in_plane))
    def _():
        sent(zsend, zs_sem)

    @pl.when(in_plane)
    def _():
        arrived(zsend.at[pl.ds(0, 7)], rr_sem)

    @pl.when(jnp.logical_not(in_plane))
    def _():
        arrived(zsend, rr_sem)


def time_kernel(m_ref, basis, out, by_cf, timed, o_sem):
    for freq in range(FREQ):
        for part in range(2):
            by_cf[pl.ds((part * FREQ + freq) * 16, 16)] = m_ref[freq, part].astype(F32)
    high, low = split_in_two(basis[...] * (1.0 / math.sqrt(FREQ)))
    weights = jnp.concatenate([high, low])
    pieces = o_sem.shape[0]
    width = 16 // pieces

    def store(piece):
        rows = pl.ds(piece * width, width)
        return pltpu.make_async_copy(timed.at[:, rows], out.at[:, rows], o_sem.at[piece])

    for piece in range(pieces):
        for s in range(piece * width, (piece + 1) * width):
            rows = by_cf[pl.ds(s, 16, stride=16), :].astype(BF16)
            rows = jnp.concatenate([rows, rows])
            values = lax.dot_general(rows, weights, (((0,), (0,)), ((), ())), preferred_element_type=F32)
            timed[:, s] = values.astype(BF16).reshape(4, 32, timed.shape[-1])
        store(piece).start()
    for piece in range(pieces):
        store(piece).wait()


def on_device(traces, taper_weights):
    shots, receivers, samples = traces.shape
    table = fourier_table(samples)
    vmem, anywhere = pl.BlockSpec(memory_space=pltpu.VMEM), pl.BlockSpec(memory_space=pl.ANY)
    dma = pltpu.SemaphoreType.DMA
    product = pl.pallas_call(
        product_kernel,
        out_shape=jax.ShapeDtypeStruct((FREQ, 2, 16, 128), BF16),
        in_specs=[anywhere, anywhere],
        out_specs=anywhere,
        scratch_shapes=[
            pltpu.VMEM((4, 16, receivers, samples), BF16),
            pltpu.VMEM((1, samples), F32),
            pltpu.VMEM((256, 128), F32),
            pltpu.VMEM((FREQ, 2, 16, 128), BF16),
            pltpu.VMEM((16, 2, 16, 128), BF16),
            pltpu.VMEM((4, 2, 2, 32, 128), BF16),
            pltpu.VMEM((2, 4, 2, 2, 2, 32, 128), BF16),
            pltpu.VMEM((4, 2, 2, 4, 32, 128), BF16),
            pltpu.VMEM((4, 64, 256), F32),
            pltpu.VMEM((2, 2, 64, 256), F32),
            pltpu.VMEM((2, 2, 64, 256), F32),
            pltpu.VMEM((2, 2, 64, 256), F32),
            pltpu.VMEM((16, 2, 16, 128), BF16),
            dma((4,)), dma, dma, dma, dma((4,)), dma((2,)), dma((2,)), dma, dma((2,)),
            dma((2,)), dma((2,)), dma, dma,
        ],
        compiler_params=pltpu.CompilerParams(
            collective_id=0, has_side_effects=True, vmem_limit_bytes=52 << 20
        ),
        name="product",
    )(traces.reshape(4, 16, receivers, samples), taper_weights.reshape(1, samples))
    timed = pl.pallas_call(
        time_kernel,
        out_shape=jax.ShapeDtypeStruct((4, 16, receivers, samples), BF16),
        in_specs=[vmem, vmem],
        out_specs=anywhere,
        scratch_shapes=[
            pltpu.VMEM((256, 128), F32),
            pltpu.VMEM((4, 16, receivers, samples), BF16),
            dma((4,)),
        ],
        compiler_params=pltpu.CompilerParams(vmem_limit_bytes=52 << 20),
        name="back_to_time",
    )(product, table)
    return timed.reshape(shots, receivers, samples)


def solution(mesh):
    placed = (P("shot", "rcv", None), P())
    return jax.shard_map(
        on_device, mesh=mesh, in_specs=placed, out_specs=P("shot", "rcv", None), check_vma=False
    )
```

time: 43.9 us -> 40.1 us (0.913)
  local copies, waits for them, and re-layouts: 3.03 us -> 0.69 us
  Pallas kernels: 40.7 us -> 39.2 us
    unnamed x6 -> x4, local copies, waits for them, and re-layouts: 3.03 us -> 0.69 us
    pallas_call x1, Pallas kernels: 2.63 us -> 1.69 us  [on_device(): pl.pallas_call(time_kernel, out_shape=jax.ShapeDtypeStruct((4, 16, receiv...]
    pallas_call x1, Pallas kernels: 38 us -> 37.5 us  [on_device(): pl.pallas_call(product_kernel, out_shape=jax.ShapeDtypeStruct((FREQ, 2, 1...]
where the time goes in v2:
time: 40.1 us; the launch traced here: 39.9 us
  Pallas kernels  39.2 us (98%)
  local copies, waits for them, and re-layouts  0.69 us (2%)
    pallas_call x1, Pallas kernels, on_device(): pl.pallas_call(product_kernel, out_shape=jax.ShapeDtypeStruct((FREQ, 2, 1...  37.5 us
    pallas_call x1, Pallas kernels, on_device(): pl.pallas_call(time_kernel, out_shape=jax.ShapeDtypeStruct((4, 16, receiv...  1.69 us

profile of v2, /device:TPU:1, one launch (start us, length us, event | category | flops | bytes accessed | tf_op | source)
XLA Modules:
  0.0 39.9 jit_solution(14438409059443673491)
XLA Ops:
  0.0 0.0 copy-start
  0.0 0.0 copy-start.1
  0.0 0.7 %copy-done.1 = f32[512]{0:T(512)S(1)} copy-done((f32[512]{0:T(512)S(1)}, f32[512]{0:T(512)}, u32[]{:S(2)}) %copy-start.1) | copy-done | bytes 2072
  0.7 37.5 %product.1.m_ref = bf16[8,2,16,128]{3,2,1,0:T(8,128)(2,1)S(1)} custom-call(bf16[4,16,32,512]{3,2,1,0:T(8,128)(2,1)} %bitcast.4, f32[1,512]{1,0:T(1,128)S(1)} %bitcast.3), custom_call_target="tpu_custom_call" | custom-call | tf_op jit(solution)/shard_map/product/pallas_call | solution.py:359
  38.2 0.0 copy-done
  38.2 1.7 %back_to_time.1 = bf16[4,16,32,512]{3,2,1,0:T(8,128)(2,1)} custom-call(bf16[8,2,16,128]{3,2,1,0:T(8,128)(2,1)S(1)} %product.1.m_ref, f32[16,512]{1,0:T(8,128)S(1)} %copy-done), custom_call_target="tpu_custom_call" | custom-call | tf_op jit(solution)/shard_map/back_to_time/pallas_call | solution.py:386
Async XLA Ops:
  0.0 38.2 %copy-start = (f32[16,512]{1,0:T(8,128)S(1)}, f32[16,512]{1,0:T(8,128)}, u32[]{:S(2)}) copy-start(f32[16,512]{1,0:T(8,128)} %constant.2.clone.basis) | copy-start | bytes 98308
  0.0 0.7 %copy-start.1 = (f32[512]{0:T(512)S(1)}, f32[512]{0:T(512)}, u32[]{:S(2)}) copy-start(f32[512]{0:T(512)} %param.4) | copy-start | bytes 6148

commit v3 on v2

--- a/solution.py
+++ b/solution.py
@@ -62,9 +62,9 @@
 
 
 def product_kernel(
-    traces, taper_any, m_ref,
-    tr, taper, by_s, zsend, zin, own, a_buf, b_buf, early, c_out, c_in, c_own, zret,
-    t_sem, w_sem, m_sem, zs_sem, zr_sem, as_sem, ar_sem, bs_sem, br_sem, cs_sem, cr_sem, rs_sem, rr_sem,
+    traces, taper, m_ref,
+    tr, by_s, zsend, zin, own, a_buf, b_buf, early, c_out, c_in, c_own, zret,
+    t_sem, m_sem, zs_sem, zr_sem, as_sem, ar_sem, bs_sem, br_sem, cs_sem, cr_sem, rs_sem, rr_sem,
 ):
     x, y, z, core = place()
     in_plane = z < FREQ
@@ -89,8 +89,6 @@
         rows = pl.ds(chunk * per_chunk, per_chunk)
         return pltpu.make_async_copy(traces.at[:, rows], tr.at[:, rows], t_sem.at[chunk])
 
-    load_taper = pltpu.make_async_copy(taper_any, taper, w_sem)
-    load_taper.start()
     for chunk in range(chunks):
         load(chunk).start()
 
@@ -109,9 +107,7 @@
             greet(device(x, lax.rem(y + step, 4), z, core))
         greet(device(x, y, z, 1 - core))
 
-    rows = fourier_rows(samples)
-    load_taper.wait()
-    high, low = split_in_two(rows * taper[...] / math.sqrt(samples))
+    high, low = split_in_two(fourier_rows(samples) * taper[...] / math.sqrt(samples))
     weights = jnp.concatenate([high, low])
     for s in range(0, 16, 2):
         if s % per_chunk == 0:
@@ -133,18 +129,23 @@
     def _():
         pl.semaphore_wait(barrier, 8)
 
-    others_first = (1, 7, 2, 6, 3, 5, 4)
-
-    def to_plane(step):
-        freq = lax.rem(z + step, 8)
+    def to_plane(freq):
         return remote(zsend.at[freq], zin.at[z], zs_sem, zr_sem.at[z // 4], device(x, y, freq, core))
 
-    @pl.when(jnp.logical_not(in_plane))
-    def _():
-        to_plane(0).start()
-
-    for step in others_first:
-        to_plane(step).start()
+    last_started = jnp.logical_and(z >= 8, z < 12)
+
+    @pl.when(last_started)
+    def _():
+        for freq in reversed(range(FREQ)):
+            to_plane(freq).start()
+
+    @pl.when(jnp.logical_not(last_started))
+    def _():
+        for freq in range(FREQ):
+
+            @pl.when(freq != z)
+            def _():
+                to_plane(freq).start()
 
     def product_of_plane():
         zin[z] = zsend[z]
@@ -157,7 +158,7 @@
 
         def b_copy(group, step):
             return remote(
-                own.at[group], b_buf.at[group, :, :, y], bs_sem, br_sem.at[group // 2],
+                own.at[group], b_buf.at[group, :, :, y], bs_sem, br_sem.at[jnp.maximum(group - 1, 0)],
                 device(x, lax.rem(y + step, 4), z, core),
             )
 
@@ -199,15 +200,13 @@
             def _():
                 arrived(a_buf.at[:, pl.ds(0, 2)], ar_sem.at[late])
 
-        def await_b(late):
-            arrived(a_buf.at[:, pl.ds(0, 3), 0], br_sem.at[late])
-
-        def right(part, deep):
+        def await_b(part, pieces):
+            arrived(a_buf.at[0 : pieces // 3, pl.ds(0, 3), 0], br_sem.at[part])
+
+        def right(deep, wide):
             return jnp.concatenate(
                 [
-                    jnp.concatenate(
-                        [b_buf[2 * deep + wide, part, half].reshape(128, 128) for wide in range(2)], axis=1
-                    )
+                    jnp.concatenate([b_buf[2 * deep + wide, part, half].reshape(128, 128) for part in range(2)], axis=1)
                     for half in range(2)
                 ]
             )
@@ -223,82 +222,82 @@
                 ]
             )
 
-        def multiply(upper, deep):
-            rows = left(upper, deep)
-            by_real = jnp.dot(rows, right(0, deep), preferred_element_type=F32)
-            by_imag = jnp.dot(rows, right(1, deep), preferred_element_type=F32)
+        def multiply(upper, deep, wide):
+            both = jnp.dot(left(upper, deep), right(deep, wide), preferred_element_type=F32)
+            by_real, by_imag = both[:, :128], both[:, 128:]
             out = []
             for at in (0, 128):
                 out.append(by_real[at : at + 64] - by_imag[at + 64 : at + 128])
                 out.append(by_imag[at : at + 64] + by_real[at + 64 : at + 128])
             return out
 
-        def to_partner(upper):
+        def to_partner(upper, wide):
             return remote(
-                c_out.at[upper], c_in.at[upper], cs_sem.at[upper], cr_sem.at[upper], device(x, y, z, 1 - core)
+                c_out.at[upper, wide], c_in.at[upper, wide], cs_sem, cr_sem.at[upper, wide], device(x, y, z, 1 - core)
             )
 
         def back(target):
-            return remote(
-                zret.at[target], m_ref.at[z], rs_sem, rr_sem, device(x, y, target, core)
-            )
-
-        def send_back(upper):
-            for wide in range(2):
-                group = 2 * upper + wide
-                for part in range(2):
-                    tiles = []
-                    for j in range(4):
-                        at = (upper, part, pl.ds(j * 16, 16), pl.ds(wide * 128, 128))
-                        tiles.append(c_own[at] + c_in[at])
-                    tiles = swap_quarters(tiles)
-                    for i in range(4):
-                        zret[group * 4 + i, part] = (tiles[i] * (1.0 / 32.0)).astype(BF16)
+            return remote(zret.at[target], m_ref.at[z], rs_sem, rr_sem, device(x, y, target, core))
+
+        def send_back(upper, wide):
+            arrived(c_in.at[upper, wide], cr_sem.at[upper, wide])
+            group = 2 * upper + wide
+            for part in range(2):
+                tiles = []
+                for j in range(4):
+                    at = (upper, wide, part, pl.ds(j * 16, 16))
+                    tiles.append(c_own[at] + c_in[at])
+                tiles = swap_quarters(tiles)
                 for i in range(4):
-                    target = group * 4 + i
-
-                    @pl.when(target != z)
-                    def _():
-                        back(target).start()
+                    zret[group * 4 + i, part] = (tiles[i] * (1.0 / 32.0)).astype(BF16)
+            for i in range(4):
+                target = group * 4 + i
+
+                @pl.when(target != z)
+                def _():
+                    back(target).start()
+
+        def add_up(upper, wide, first, second):
+            for part in range(2):
+                c_out[upper, wide, part] = first[part] + second[part]
+            to_partner(upper, wide).start()
+            for part in range(2):
+                c_own[upper, wide, part] = first[2 + part] + second[2 + part]
+
+        def group_at(index):
+            near = jnp.where(z < 4, 3, 2)
+            return jnp.where(index < 2, (z // 4) ^ index, jnp.where(index == 2, near, 5 - near))
 
         @pl.loop(0, 2)
         def _(index):
-            arrange((z // 4) ^ index)
+            arrange(group_at(index))
 
         await_a(0)
-        await_b(0)
-        for k, value in enumerate(multiply(0, 0)):
-            early[k] = value
-
-        @pl.loop(0, 2)
+        await_b(0, 6)
+        for wide in range(2):
+            for k, value in enumerate(multiply(0, 0, wide)):
+                early[wide, k] = value
+
+        @pl.loop(2, 4)
         def _(index):
-            arrange(2 + (1 - z // 4) ^ index)
-
-        await_b(1)
-        values = multiply(0, 1)
-        for part in range(2):
-            c_out[0, part] = early[part] + values[part]
-        to_partner(0).start()
-        for part in range(2):
-            c_own[0, part] = early[2 + part] + values[2 + part]
-        to_partner(0).wait_recv()
-        send_back(0)
+            arrange(group_at(index))
+
+        await_b(1, 3)
+        add_up(0, 0, early[0], multiply(0, 1, 0))
+        await_b(2, 3)
+        add_up(0, 1, early[1], multiply(0, 1, 1))
+        send_back(0, 0)
+        await_a(1)
+        add_up(1, 1, multiply(1, 0, 1), multiply(1, 1, 1))
+        send_back(0, 1)
         keep = pltpu.make_async_copy(zret.at[z], m_ref.at[z], m_sem)
         keep.start()
-
-        await_a(1)
-        values = [a + b for a, b in zip(multiply(1, 0), multiply(1, 1))]
-        for part in range(2):
-            c_out[1, part] = values[part]
-        to_partner(1).start()
-        for part in range(2):
-            c_own[1, part] = values[2 + part]
-        to_partner(1).wait_recv()
-        send_back(1)
+        add_up(1, 0, multiply(1, 0, 0), multiply(1, 1, 0))
+        send_back(1, 1)
+        send_back(1, 0)
 
         keep.wait()
-        to_partner(0).wait_send()
-        to_partner(1).wait_send()
+        sent(c_out, cs_sem)
         sent(a_buf.at[:, pl.ds(0, 3)], as_sem.at[0])
         sent(a_buf.at[:, pl.ds(0, 3)], bs_sem)
 
@@ -359,24 +358,23 @@
     product = pl.pallas_call(
         product_kernel,
         out_shape=jax.ShapeDtypeStruct((FREQ, 2, 16, 128), BF16),
-        in_specs=[anywhere, anywhere],
+        in_specs=[anywhere, vmem],
         out_specs=anywhere,
         scratch_shapes=[
             pltpu.VMEM((4, 16, receivers, samples), BF16),
-            pltpu.VMEM((1, samples), F32),
             pltpu.VMEM((256, 128), F32),
             pltpu.VMEM((FREQ, 2, 16, 128), BF16),
             pltpu.VMEM((16, 2, 16, 128), BF16),
             pltpu.VMEM((4, 2, 2, 32, 128), BF16),
             pltpu.VMEM((2, 4, 2, 2, 2, 32, 128), BF16),
             pltpu.VMEM((4, 2, 2, 4, 32, 128), BF16),
-            pltpu.VMEM((4, 64, 256), F32),
-            pltpu.VMEM((2, 2, 64, 256), F32),
-            pltpu.VMEM((2, 2, 64, 256), F32),
-            pltpu.VMEM((2, 2, 64, 256), F32),
+            pltpu.VMEM((2, 4, 64, 128), F32),
+            pltpu.VMEM((2, 2, 2, 64, 128), F32),
+            pltpu.VMEM((2, 2, 2, 64, 128), F32),
+            pltpu.VMEM((2, 2, 2, 64, 128), F32),
             pltpu.VMEM((16, 2, 16, 128), BF16),
-            dma((4,)), dma, dma, dma, dma((4,)), dma((2,)), dma((2,)), dma, dma((2,)),
-            dma((2,)), dma((2,)), dma, dma,
+            dma((4,)), dma, dma, dma((4,)), dma((2,)), dma((2,)), dma, dma((3,)),
+            dma, dma((2, 2)), dma, dma,
         ],
         compiler_params=pltpu.CompilerParams(
             collective_id=0, has_side_effects=True, vmem_limit_bytes=52 << 20

time: 40.1 us -> 39.3 us (0.980)
  Pallas kernels: 39.2 us -> 38.4 us
    pallas_call x1, Pallas kernels: 37.5 us -> 36.7 us  [on_device(): pl.pallas_call(product_kernel, out_shape=jax.ShapeDtypeStruct((FREQ, 2, 1...]
where the time goes in v3:
time: 39.3 us; the launch traced here: 39.1 us
  Pallas kernels  38.4 us (98%)
  local copies, waits for them, and re-layouts  0.69 us (2%)
    pallas_call x1, Pallas kernels, on_device(): pl.pallas_call(product_kernel, out_shape=jax.ShapeDtypeStruct((FREQ, 2, 1...  36.7 us
    pallas_call x1, Pallas kernels, on_device(): pl.pallas_call(time_kernel, out_shape=jax.ShapeDtypeStruct((4, 16, receiv...  1.69 us

profile of v3, /device:TPU:1, one launch (start us, length us, event | category | flops | bytes accessed | tf_op | source)
XLA Modules:
  0.0 39.1 jit_solution(16141007212754822832)
XLA Ops:
  0.0 0.0 copy-start
  0.0 0.0 copy-start.1
  0.0 0.7 %copy-done.1 = f32[512]{0:T(512)S(1)} copy-done((f32[512]{0:T(512)S(1)}, f32[512]{0:T(512)}, u32[]{:S(2)}) %copy-start.1) | copy-done | bytes 2072
  0.7 36.7 %product.1.m_ref = bf16[8,2,16,128]{3,2,1,0:T(8,128)(2,1)S(1)} custom-call(bf16[4,16,32,512]{3,2,1,0:T(8,128)(2,1)} %bitcast.4, f32[1,512]{1,0:T(1,128)S(1)} %bitcast.3), custom_call_target="tpu_custom_call" | custom-call | tf_op jit(solution)/shard_map/product/pallas_call | solution.py:358
  37.4 0.0 copy-done
  37.4 1.7 %back_to_time.1 = bf16[4,16,32,512]{3,2,1,0:T(8,128)(2,1)} custom-call(bf16[8,2,16,128]{3,2,1,0:T(8,128)(2,1)S(1)} %product.1.m_ref, f32[16,512]{1,0:T(8,128)S(1)} %copy-done), custom_call_target="tpu_custom_call" | custom-call | tf_op jit(solution)/shard_map/back_to_time/pallas_call | solution.py:384
Async XLA Ops:
  0.0 37.4 %copy-start = (f32[16,512]{1,0:T(8,128)S(1)}, f32[16,512]{1,0:T(8,128)}, u32[]{:S(2)}) copy-start(f32[16,512]{1,0:T(8,128)} %constant.2.clone.basis) | copy-start | bytes 98308
  0.0 0.7 %copy-start.1 = (f32[512]{0:T(512)S(1)}, f32[512]{0:T(512)}, u32[]{:S(2)}) copy-start(f32[512]{0:T(512)} %param.4) | copy-start | bytes 6148

commit v4 on v3

--- a/solution.py
+++ b/solution.py
@@ -63,7 +63,7 @@
 
 def product_kernel(
     traces, taper, m_ref,
-    tr, by_s, zsend, zin, own, a_buf, b_buf, early, c_out, c_in, c_own, zret,
+    tr, by_s, zsend, zin, own, a_buf, b_buf, c_out, c_in, c_own, zret,
     t_sem, m_sem, zs_sem, zr_sem, as_sem, ar_sem, bs_sem, br_sem, cs_sem, cr_sem, rs_sem, rr_sem,
 ):
     x, y, z, core = place()
@@ -158,7 +158,7 @@
 
         def b_copy(group, step):
             return remote(
-                own.at[group], b_buf.at[group, :, :, y], bs_sem, br_sem.at[jnp.maximum(group - 1, 0)],
+                own.at[group], b_buf.at[group, :, :, y], bs_sem, br_sem.at[group],
                 device(x, lax.rem(y + step, 4), z, core),
             )
 
@@ -178,18 +178,21 @@
                     rows = pl.ds(j % 2 * 16, 16)
                     own[group, part, j // 2, rows] = tile
                     b_buf[group, part, j // 2, y, rows] = tile
+        def send_a(group):
+            for step in (2, 1, 3):
+                a_copy(group, step).start()
+
+            @pl.when(x_core != core)
+            def _():
+                a_copy(group, 0).start()
+
+            @pl.when(x_core == core)
+            def _():
+                a_buf[x_half, group, core] = own[group]
+
+        def send_b(group):
             for step in (2, 1, 3):
                 b_copy(group, step).start()
-            for step in (2, 1, 3):
-                a_copy(group, step).start()
-
-            @pl.when(x_core != core)
-            def _():
-                a_copy(group, 0).start()
-
-            @pl.when(x_core == core)
-            def _():
-                a_buf[x_half, group, core] = own[group]
 
         def await_a(late):
             @pl.when(x_core == core)
@@ -200,8 +203,8 @@
             def _():
                 arrived(a_buf.at[:, pl.ds(0, 2)], ar_sem.at[late])
 
-        def await_b(part, pieces):
-            arrived(a_buf.at[0 : pieces // 3, pl.ds(0, 3), 0], br_sem.at[part])
+        def await_b(group):
+            arrived(a_buf.at[0, pl.ds(0, 3), 0], br_sem.at[group])
 
         def right(deep, wide):
             return jnp.concatenate(
@@ -265,36 +268,50 @@
                 c_own[upper, wide, part] = first[2 + part] + second[2 + part]
 
         def group_at(index):
-            near = jnp.where(z < 4, 3, 2)
+            near = 2
             return jnp.where(index < 2, (z // 4) ^ index, jnp.where(index == 2, near, 5 - near))
 
         @pl.loop(0, 2)
         def _(index):
-            arrange(group_at(index))
-
-        await_a(0)
-        await_b(0, 6)
-        for wide in range(2):
-            for k, value in enumerate(multiply(0, 0, wide)):
-                early[wide, k] = value
+            group = group_at(index)
+            arrange(group)
+
+            @pl.when(group == 0)
+            def _():
+                send_b(group)
+
+            send_a(group)
 
         @pl.loop(2, 4)
         def _(index):
-            arrange(group_at(index))
-
-        await_b(1, 3)
-        add_up(0, 0, early[0], multiply(0, 1, 0))
-        await_b(2, 3)
-        add_up(0, 1, early[1], multiply(0, 1, 1))
+            group = group_at(index)
+            arrange(group)
+
+            @pl.when(group == 2)
+            def _():
+                send_b(group)
+
+        for group in (2, 3):
+            send_a(group)
+        for group in (1, 3):
+            send_b(group)
+
+        await_a(0)
+        await_b(0)
+        await_b(2)
+        add_up(0, 0, multiply(0, 0, 0), multiply(0, 1, 0))
         send_back(0, 0)
         await_a(1)
+        add_up(1, 0, multiply(1, 0, 0), multiply(1, 1, 0))
+        await_b(1)
+        await_b(3)
         add_up(1, 1, multiply(1, 0, 1), multiply(1, 1, 1))
+        send_back(1, 0)
+        add_up(0, 1, multiply(0, 0, 1), multiply(0, 1, 1))
+        send_back(1, 1)
         send_back(0, 1)
         keep = pltpu.make_async_copy(zret.at[z], m_ref.at[z], m_sem)
         keep.start()
-        add_up(1, 0, multiply(1, 0, 0), multiply(1, 1, 0))
-        send_back(1, 1)
-        send_back(1, 0)
 
         keep.wait()
         sent(c_out, cs_sem)
@@ -368,12 +385,11 @@
             pltpu.VMEM((4, 2, 2, 32, 128), BF16),
             pltpu.VMEM((2, 4, 2, 2, 2, 32, 128), BF16),
             pltpu.VMEM((4, 2, 2, 4, 32, 128), BF16),
-            pltpu.VMEM((2, 4, 64, 128), F32),
             pltpu.VMEM((2, 2, 2, 64, 128), F32),
             pltpu.VMEM((2, 2, 2, 64, 128), F32),
             pltpu.VMEM((2, 2, 2, 64, 128), F32),
             pltpu.VMEM((16, 2, 16, 128), BF16),
-            dma((4,)), dma, dma, dma((4,)), dma((2,)), dma((2,)), dma, dma((3,)),
+            dma((4,)), dma, dma, dma((4,)), dma((2,)), dma((2,)), dma, dma((4,)),
             dma, dma((2, 2)), dma, dma,
         ],
         compiler_params=pltpu.CompilerParams(

time: 39.3 us -> 37.1 us (0.944)
  the two profiles are of different devices: /device:TPU:1 before, /device:TPU:448 now
where the time goes in v4:
time: 37.1 us; the launch traced here: 36.9 us
  Pallas kernels  36.1 us (97%)
  local copies, waits for them, and re-layouts  0.69 us (2%)
    pallas_call x1, Pallas kernels, on_device(): pl.pallas_call(product_kernel, out_shape=jax.ShapeDtypeStruct((FREQ, 2, 1...  34.5 us
    pallas_call x1, Pallas kernels, on_device(): pl.pallas_call(time_kernel, out_shape=jax.ShapeDtypeStruct((4, 16, receiv...  1.69 us

profile of v4, /device:TPU:448, one launch (start us, length us, event | category | flops | bytes accessed | tf_op | source)
XLA Modules:
  0.0 36.9 jit_solution(13107310026554951313)
XLA Ops:
  0.0 0.0 copy-start
  0.0 0.0 copy-start.1
  0.0 0.7 %copy-done.1 = f32[512]{0:T(512)S(1)} copy-done((f32[512]{0:T(512)S(1)}, f32[512]{0:T(512)}, u32[]{:S(2)}) %copy-start.1) | copy-done | bytes 2072
  0.7 34.5 %product.1.m_ref = bf16[8,2,16,128]{3,2,1,0:T(8,128)(2,1)S(1)} custom-call(bf16[4,16,32,512]{3,2,1,0:T(8,128)(2,1)} %bitcast.4, f32[1,512]{1,0:T(1,128)S(1)} %bitcast.3), custom_call_target="tpu_custom_call" | custom-call | tf_op jit(solution)/shard_map/product/pallas_call | solution.py:375
  35.2 0.0 copy-done
  35.2 1.7 %back_to_time.1 = bf16[4,16,32,512]{3,2,1,0:T(8,128)(2,1)} custom-call(bf16[8,2,16,128]{3,2,1,0:T(8,128)(2,1)S(1)} %product.1.m_ref, f32[16,512]{1,0:T(8,128)S(1)} %copy-done), custom_call_target="tpu_custom_call" | custom-call | tf_op jit(solution)/shard_map/back_to_time/pallas_call | solution.py:400
Async XLA Ops:
  0.0 35.2 %copy-start = (f32[16,512]{1,0:T(8,128)S(1)}, f32[16,512]{1,0:T(8,128)}, u32[]{:S(2)}) copy-start(f32[16,512]{1,0:T(8,128)} %constant.2.clone.basis) | copy-start | bytes 98308
  0.0 0.7 %copy-start.1 = (f32[512]{0:T(512)S(1)}, f32[512]{0:T(512)}, u32[]{:S(2)}) copy-start(f32[512]{0:T(512)} %param.4) | copy-start | bytes 6148

commit v5 on v4

--- a/solution.py
+++ b/solution.py
@@ -132,20 +132,11 @@
     def to_plane(freq):
         return remote(zsend.at[freq], zin.at[z], zs_sem, zr_sem.at[z // 4], device(x, y, freq, core))
 
-    last_started = jnp.logical_and(z >= 8, z < 12)
-
-    @pl.when(last_started)
-    def _():
-        for freq in reversed(range(FREQ)):
+    for freq in range(FREQ):
+
+        @pl.when(freq != z)
+        def _():
             to_plane(freq).start()
-
-    @pl.when(jnp.logical_not(last_started))
-    def _():
-        for freq in range(FREQ):
-
-            @pl.when(freq != z)
-            def _():
-                to_plane(freq).start()
 
     def product_of_plane():
         zin[z] = zsend[z]
@@ -267,13 +258,9 @@
             for part in range(2):
                 c_own[upper, wide, part] = first[2 + part] + second[2 + part]
 
-        def group_at(index):
-            near = 2
-            return jnp.where(index < 2, (z // 4) ^ index, jnp.where(index == 2, near, 5 - near))
-
         @pl.loop(0, 2)
         def _(index):
-            group = group_at(index)
+            group = (z // 4) ^ index
             arrange(group)
 
             @pl.when(group == 0)
@@ -282,33 +269,38 @@
 
             send_a(group)
 
-        @pl.loop(2, 4)
-        def _(index):
-            group = group_at(index)
-            arrange(group)
-
-            @pl.when(group == 2)
-            def _():
-                send_b(group)
-
-        for group in (2, 3):
-            send_a(group)
-        for group in (1, 3):
-            send_b(group)
+        arrange(2)
+        send_b(2)
+        send_a(2)
+        send_b(1)
+        arrange(3)
+        send_a(3)
+        send_b(3)
 
         await_a(0)
         await_b(0)
         await_b(2)
         add_up(0, 0, multiply(0, 0, 0), multiply(0, 1, 0))
         send_back(0, 0)
+        far = jnp.where(z >= 6, 1, 0)
         await_a(1)
-        add_up(1, 0, multiply(1, 0, 0), multiply(1, 1, 0))
-        await_b(1)
-        await_b(3)
-        add_up(1, 1, multiply(1, 0, 1), multiply(1, 1, 1))
-        send_back(1, 0)
+
+        @pl.when(far == 1)
+        def _():
+            await_b(1)
+            await_b(3)
+
+        add_up(1, far, multiply(1, 0, far), multiply(1, 1, far))
+
+        @pl.when(far == 0)
+        def _():
+            await_b(1)
+            await_b(3)
+
+        add_up(1, 1 - far, multiply(1, 0, 1 - far), multiply(1, 1, 1 - far))
+        send_back(1, far)
         add_up(0, 1, multiply(0, 0, 1), multiply(0, 1, 1))
-        send_back(1, 1)
+        send_back(1, 1 - far)
         send_back(0, 1)
         keep = pltpu.make_async_copy(zret.at[z], m_ref.at[z], m_sem)
         keep.start()

time: 37.1 us -> 36.3 us (0.978)
  the two profiles are of different devices: /device:TPU:448 before, /device:TPU:1 now
where the time goes in v5:
time: 36.3 us; the launch traced here: 36 us
  Pallas kernels  35.3 us (97%)
  local copies, waits for them, and re-layouts  0.69 us (2%)
    pallas_call x1, Pallas kernels, on_device(): pl.pallas_call(product_kernel, out_shape=jax.ShapeDtypeStruct((FREQ, 2, 1...  33.6 us
    pallas_call x1, Pallas kernels, on_device(): pl.pallas_call(time_kernel, out_shape=jax.ShapeDtypeStruct((4, 16, receiv...  1.69 us

profile of v5, /device:TPU:1, one launch (start us, length us, event | category | flops | bytes accessed | tf_op | source)
XLA Modules:
  0.0 36.0 jit_solution(4837595512463419222)
XLA Ops:
  0.0 0.0 copy-start
  0.0 0.0 copy-start.1
  0.0 0.7 %copy-done.1 = f32[512]{0:T(512)S(1)} copy-done((f32[512]{0:T(512)S(1)}, f32[512]{0:T(512)}, u32[]{:S(2)}) %copy-start.1) | copy-done | bytes 2072
  0.7 33.6 %product.1.m_ref = bf16[8,2,16,128]{3,2,1,0:T(8,128)(2,1)S(1)} custom-call(bf16[4,16,32,512]{3,2,1,0:T(8,128)(2,1)} %bitcast.4, f32[1,512]{1,0:T(1,128)S(1)} %bitcast.3), custom_call_target="tpu_custom_call" | custom-call | tf_op jit(solution)/shard_map/product/pallas_call | solution.py:367
  34.3 0.0 copy-done
  34.3 1.7 %back_to_time.1 = bf16[4,16,32,512]{3,2,1,0:T(8,128)(2,1)} custom-call(bf16[8,2,16,128]{3,2,1,0:T(8,128)(2,1)S(1)} %product.1.m_ref, f32[16,512]{1,0:T(8,128)S(1)} %copy-done), custom_call_target="tpu_custom_call" | custom-call | tf_op jit(solution)/shard_map/back_to_time/pallas_call | solution.py:392
Async XLA Ops:
  0.0 34.3 %copy-start = (f32[16,512]{1,0:T(8,128)S(1)}, f32[16,512]{1,0:T(8,128)}, u32[]{:S(2)}) copy-start(f32[16,512]{1,0:T(8,128)} %constant.2.clone.basis) | copy-start | bytes 98308
  0.0 0.7 %copy-start.1 = (f32[512]{0:T(512)S(1)}, f32[512]{0:T(512)}, u32[]{:S(2)}) copy-start(f32[512]{0:T(512)} %param.4) | copy-start | bytes 6148

commit v6 on v5

--- a/solution.py
+++ b/solution.py
@@ -279,8 +279,9 @@
 
         await_a(0)
         await_b(0)
+        first = multiply(0, 0, 0)
         await_b(2)
-        add_up(0, 0, multiply(0, 0, 0), multiply(0, 1, 0))
+        add_up(0, 0, first, multiply(0, 1, 0))
         send_back(0, 0)
         far = jnp.where(z >= 6, 1, 0)
         await_a(1)
@@ -381,7 +382,7 @@
             pltpu.VMEM((2, 2, 2, 64, 128), F32),
             pltpu.VMEM((2, 2, 2, 64, 128), F32),
             pltpu.VMEM((16, 2, 16, 128), BF16),
-            dma((4,)), dma, dma, dma((4,)), dma((2,)), dma((2,)), dma, dma((4,)),
+            dma((2,)), dma, dma, dma((4,)), dma((2,)), dma((2,)), dma, dma((4,)),
             dma, dma((2, 2)), dma, dma,
         ],
         compiler_params=pltpu.CompilerParams(

time: 36.3 us -> 36.3 us (level)
  no operation moved by 1% of the time
where the time goes in v6:
time: 36.3 us; the launch traced here: 35.9 us
  Pallas kernels  35.2 us (97%)
  local copies, waits for them, and re-layouts  0.69 us (2%)
    pallas_call x1, Pallas kernels, on_device(): pl.pallas_call(product_kernel, out_shape=jax.ShapeDtypeStruct((FREQ, 2, 1...  33.5 us
    pallas_call x1, Pallas kernels, on_device(): pl.pallas_call(time_kernel, out_shape=jax.ShapeDtypeStruct((4, 16, receiv...  1.69 us

profile of v6, /device:TPU:1, one launch (start us, length us, event | category | flops | bytes accessed | tf_op | source)
XLA Modules:
  0.0 35.9 jit_solution(14510391516302090446)
XLA Ops:
  0.0 0.0 copy-start
  0.0 0.0 copy-start.1
  0.0 0.7 %copy-done.1 = f32[512]{0:T(512)S(1)} copy-done((f32[512]{0:T(512)S(1)}, f32[512]{0:T(512)}, u32[]{:S(2)}) %copy-start.1) | copy-done | bytes 2072
  0.7 33.5 %product.1.m_ref = bf16[8,2,16,128]{3,2,1,0:T(8,128)(2,1)S(1)} custom-call(bf16[4,16,32,512]{3,2,1,0:T(8,128)(2,1)} %bitcast.4, f32[1,512]{1,0:T(1,128)S(1)} %bitcast.3), custom_call_target="tpu_custom_call" | custom-call | tf_op jit(solution)/shard_map/product/pallas_call | solution.py:368
  34.2 0.0 copy-done
  34.2 1.7 %back_to_time.1 = bf16[4,16,32,512]{3,2,1,0:T(8,128)(2,1)} custom-call(bf16[8,2,16,128]{3,2,1,0:T(8,128)(2,1)S(1)} %product.1.m_ref, f32[16,512]{1,0:T(8,128)S(1)} %copy-done), custom_call_target="tpu_custom_call" | custom-call | tf_op jit(solution)/shard_map/back_to_time/pallas_call | solution.py:393
Async XLA Ops:
  0.0 34.2 %copy-start = (f32[16,512]{1,0:T(8,128)S(1)}, f32[16,512]{1,0:T(8,128)}, u32[]{:S(2)}) copy-start(f32[16,512]{1,0:T(8,128)} %constant.2.clone.basis) | copy-start | bytes 98308
  0.0 0.7 %copy-start.1 = (f32[512]{0:T(512)S(1)}, f32[512]{0:T(512)}, u32[]{:S(2)}) copy-start(f32[512]{0:T(512)} %param.4) | copy-start | bytes 6148
